TPU v7x, 128 devices: a whole 4x4x4 slice. The times are simulated.
128 devices in a mesh: lat: 8 (over z_hi, x), lon: 16 (over y, z_lo, core).
Axes of the slice: x: 4, y: 4, z: 4 (z_hi: 2, z_lo: 2; z = z_hi * 2 + z_lo), core: 2. Of those that a mesh axis runs over, the one named last changes fastest.
Arguments:
- fine_tokens: bfloat16 [8, 4, 48, 192, 512], P(None, None, 'lat', 'lon'), may hold values from -40 to 40
- gain_fine: float32 [512], replicated, may hold values from 0.1 to 1.9
- w_qkv_fine: bfloat16 [512, 1536], replicated, may hold values from -0.25 to 0.25
- bias_fine: float32 [8, 144, 144], replicated, may hold values from -4 to 220
- w_out_fine: bfloat16 [512, 512], replicated, may hold values from -0.25 to 0.25
- gain_merge: float32 [2048], replicated, may hold values from 0.1 to 1.9
- w_merge: bfloat16 [2048, 1024], replicated, may hold values from -0.125 to 0.125
- gain_coarse: float32 [1024], replicated, may hold values from 0.1 to 1.9
- w_qkv_coarse: bfloat16 [1024, 3072], replicated, may hold values from -0.1875 to 0.1875
- bias_coarse: float32 [16, 144, 144], replicated, may hold values from -4 to 220
- w_out_coarse: bfloat16 [1024, 1024], replicated, may hold values from -0.1875 to 0.1875
Outputs:
- fine_out: float32 [8, 4, 48, 192, 512], P(None, None, 'lat', 'lon')
- coarse_out: float32 [8, 4, 24, 96, 1024], P(None, None, 'lat', 'lon')
All inputs are finite; a program needn't handle non-finite values.
Results may differ from a plain program's by a relative error of at most 0.012.
Values may be sent and summed in bfloat16 or wider, within the bound.
A program may use at most 192 MiB of HBM per device.

v0:
```python
import functools

import jax
import jax.numpy as jnp
import numpy as np
from jax import lax
from jax.experimental import pallas as pl
from jax.experimental.pallas import tpu as pltpu
from jax.sharding import PartitionSpec as P

EPS = 1e-05
NEG = -1e30
ROWS, COLS, WLEV, HS = 6, 12, 2, 64
HALF_R, HALF_C = ROWS // 2, COLS // 2
WIN = WLEV * ROWS * COLS
QUART = WLEV * HALF_R * HALF_C
STEP = 32
PIECE = 48
NW = 4
CROWS = NW * QUART
NAT = WLEV * ROWS * 16
D1, D2 = 512, 1024
IN_TILE = (0, 1, 2, 3)
IN_WINDOW = (3, 2, 1, 0)
TO_QUART, TO_GROUP, TO_WIN, HEADS_GROUP, HEADS_NAT, FROM_WIN = range(6)
MESH = pl.DeviceIdType.MESH
VMEM_LIMIT = 58 * 1024 * 1024


def row_maps():
    maps = np.zeros((6, NW, 4 * PIECE, 4 * PIECE), np.float32)
    for w in range(NW):
        shift = 4 * w
        for lev in range(WLEV):
            for r in range(ROWS):
                for c in range(COLS):
                    nat = (lev * ROWS + r) * 16 + c
                    win = lev * ROWS * COLS + r * COLS + c
                    q = (r // HALF_R) * 2 + c // HALF_C
                    t = lev * 18 + (r % HALF_R) * HALF_C + c % HALF_C
                    qp = q * PIECE + shift + t
                    g = (c % 2) * 2 + r % 2
                    gp = g * PIECE + shift + lev * 18 + (r // 2) * HALF_C + c // 2
                    maps[TO_QUART, w, qp, nat] = 1
                    maps[TO_GROUP, w, gp, nat] = 1
                    maps[TO_WIN, w, win, qp] = 1
                    maps[HEADS_GROUP, w, gp, qp] = 1
                    maps[HEADS_NAT, w, nat, qp] = 1
                    maps[FROM_WIN, w, qp, win] = 1
    return maps


def spread_map():
    spread = np.zeros((NW * WLEV * HALF_R * 8, CROWS), np.float32)
    for block in range(NW * WLEV * HALF_R):
        for j in range(HALF_C):
            spread[block * 8 + j, block * HALF_C + j] = 1
    return spread


def dot(a, b):
    return jnp.dot(a, b, preferred_element_type=jnp.float32)


def dot_t(a, b):
    return lax.dot_general(a, b, (((1,), (1,)), ((), ())), preferred_element_type=jnp.float32)


def normed(values, gain):
    average = jnp.mean(values, axis=-1, keepdims=True)
    centred = values - average
    variance = jnp.mean(centred * centred, axis=-1, keepdims=True)
    return (centred * lax.rsqrt(variance + EPS) * gain).astype(jnp.bfloat16)


def assemble(piece):
    blocks = []
    for n in range(9):
        w, part = divmod(n, 2)
        if w == NW:
            w, part = NW - 1, 2
        block = piece(w)[part * 16 : part * 16 + 16]
        if part == 0 and w > 0:
            block = block + piece(w - 1)[32:48]
        blocks.append(block)
    return jnp.concatenate(blocks, axis=0)


def attend_pair(query, key, value, bias0, bias1):
    low = lax.broadcasted_iota(jnp.int32, (WIN, 128), 1) < HS
    one = jnp.ones((), jnp.bfloat16)
    zero = jnp.zeros((), jnp.bfloat16)
    results = []
    for side, bias in ((low, bias0), (jnp.logical_not(low), bias1)):
        scores = dot_t(jnp.where(side, query, zero), key) + bias
        top = jnp.max(scores, axis=-1, keepdims=True)
        probs = jnp.exp(scores - top).astype(jnp.bfloat16)
        results.append(dot(probs, jnp.where(side, value, one)))
    total = jnp.where(low, results[0], results[1])
    weight = pltpu.roll(jnp.where(low, results[1], results[0]), HS, 1)
    return (total / weight).astype(jnp.bfloat16)


def main_kernel(
    n_chunks,
    n_lat,
    n_lon,
    tokens_hbm,
    gain_fine,
    w_qkv_fine_hbm,
    bias_fine_hbm,
    w_out_fine_hbm,
    gain_merge,
    w_merge_hbm,
    gain_coarse,
    w_qkv_coarse_hbm,
    bias_coarse_hbm,
    maps_hbm,
    heads_nat_hbm,
    coarse_in_hbm,
    heads_coarse_hbm,
    tokens,
    w_qkv_fine,
    bias_fine,
    w_out_fine,
    w_merge,
    w_qkv_coarse,
    bias_coarse,
    maps,
    padded,
    pieces,
    fine_send,
    fine_recv,
    xn,
    qkv,
    heads_send,
    heads_recv,
    group_heads,
    fine_rows,
    heads_nat,
    coarse_in,
    coarse_recv,
    xn_coarse,
    qkv_coarse,
    back_send,
    back_recv,
    heads_coarse,
    load_sem,
    token_sem,
    fine_ssem,
    fine_rsem,
    heads_ssem,
    heads_rsem,
    coarse_ssem,
    coarse_rsem,
    back_ssem,
    back_rsem,
    out_sem,
):
    lat = lax.axis_index("lat")
    lon = lax.axis_index("lon")
    member = (lat % 2) * 2 + lon % 2

    def at(dlat, dlon):
        return (lax.rem(lat + dlat + n_lat, n_lat), lax.rem(lon + dlon + n_lon, n_lon))

    def partner(k):
        return (
            lat + (k // 2) * (1 - 2 * (lat % 2)),
            lon + (k % 2) * (1 - 2 * (lon % 2)),
        )

    def load(n, src, dst):
        return pltpu.make_async_copy(src, dst, load_sem.at[n])

    loads = [
        load(0, maps_hbm, maps),
        load(1, w_qkv_fine_hbm, w_qkv_fine),
        load(2, bias_fine_hbm, bias_fine.at[0]),
        load(3, w_out_fine_hbm, w_out_fine),
        load(4, w_merge_hbm, w_merge),
        load(5, w_qkv_coarse_hbm, w_qkv_coarse),
        load(6, bias_coarse_hbm, bias_coarse),
    ]
    token_loads = [
        pltpu.make_async_copy(
            tokens_hbm.at[pl.ds(2 * c, 2)], tokens.at[c], token_sem.at[c]
        )
        for c in range(n_chunks)
    ]
    token_loads[0].start()
    loads[0].start()
    for copy in token_loads[1:]:
        copy.start()
    for copy in loads[1:]:
        copy.start()

    barrier = pltpu.get_barrier_semaphore()
    for near in (at(0, -1), at(0, 1), at(-1, 0), at(1, 0), at(-1, -1), at(1, 1), partner(3)):
        pl.semaphore_signal(barrier, inc=1, device_id=near, device_id_type=MESH)
    padded[...] = jnp.zeros_like(padded)
    pl.semaphore_wait(barrier, 7)
    loads[0].wait()

    def way(c):
        return 2 * (c % 2) - 1

    def quarter(c, k):
        return 3 - k + (c % 2) * (2 * k - 3)

    def fine_copy(c, k):
        q = quarter(c, k)
        return pltpu.make_async_remote_copy(
            fine_send.at[c, q],
            fine_recv.at[c, q],
            fine_ssem.at[c, k],
            fine_rsem.at[c, k],
            device_id=at(k // 2 * way(c), k % 2 * way(c)),
            device_id_type=MESH,
        )

    def heads_copy(c, k):
        q = quarter(c, k)
        return pltpu.make_async_remote_copy(
            heads_send.at[c, q],
            heads_recv.at[c, q],
            heads_ssem.at[c, k],
            heads_rsem.at[c, k],
            device_id=at(-(k // 2) * way(c), -(k % 2) * way(c)),
            device_id_type=MESH,
        )

    def other(k):
        mine_lat, mine_lon = lat % 2, lon % 2
        to_lat = mine_lat + (k // 2) * (1 - 2 * mine_lat)
        to_lon = mine_lon + (k % 2) * (1 - 2 * mine_lon)
        return to_lat * 2 + to_lon

    def coarse_copy(c, k):
        start = pl.multiple_of(other(k) * STEP, STEP)
        return pltpu.make_async_remote_copy(
            coarse_in.at[c, pl.ds(start, PIECE)],
            coarse_recv.at[c, member],
            coarse_ssem.at[c, k],
            coarse_rsem.at[c, k],
            device_id=partner(k),
            device_id_type=MESH,
        )

    def back_copy(c, k):
        return pltpu.make_async_remote_copy(
            back_send.at[c, other(k)],
            back_recv.at[c, member],
            back_ssem.at[c, k],
            back_rsem.at[c, k],
            device_id=partner(k),
            device_id_type=MESH,
        )

    def nat_rows(c, w):
        return padded[c, pl.ds(w * WLEV * ROWS, WLEV * ROWS)].reshape(NAT, D1)

    def quart_rows(ref, c, w, order):
        start = pl.multiple_of(w * STEP, STEP)
        return jnp.concatenate([ref[c, q, pl.ds(start, PIECE)] for q in order], axis=0)

    def put_quarters(c, send, recv, order):
        for n, q in enumerate(order):
            send[c, q] = assemble(lambda w: pieces[w, pl.ds(n * PIECE, PIECE)])
        own = quarter(c, 0)
        recv[c, own] = send[c, own]

    def send_tokens(c, _):
        for n in range(n_chunks):

            @pl.when(c == n)
            def _():
                token_loads[n].wait()

        block = tokens[c].reshape(2 * 4 * ROWS, COLS, D1)
        padded[c, :, pl.ds(0, COLS)] = block

        def one(w, _):
            pieces[w] = dot(maps[TO_QUART, w], nat_rows(c, w)).astype(jnp.bfloat16)
            return 0

        lax.fori_loop(0, NW, one, 0)
        put_quarters(c, fine_send, fine_recv, IN_TILE)
        for k in range(1, 4):
            fine_copy(c, k).start()
        return 0

    lax.fori_loop(0, n_chunks, send_tokens, 0)

    loads[1].wait()
    loads[2].wait()
    token_q = lax.broadcasted_iota(jnp.int32, (WIN, WIN), 0)
    token_k = lax.broadcasted_iota(jnp.int32, (WIN, WIN), 1)
    late_q = (token_q % (ROWS * COLS)) >= HALF_R * COLS
    late_k = (token_k % (ROWS * COLS)) >= HALF_R * COLS
    mask = jnp.where(late_q == late_k, 0.0, NEG)
    for h in range(D1 // HS):
        bias_fine[1, h] = bias_fine[0, h] + mask
    loads[3].wait()
    loads[4].wait()
    loads[5].wait()
    loads[6].wait()

    def fine_attention(c):
        for k in range(1, 4):
            fine_copy(c, k).wait_recv()

        def gather(w, _):
            rows = dot(maps[TO_WIN, w][:WIN], quart_rows(fine_recv, c, w, IN_WINDOW))
            start = pl.multiple_of(w * WIN, 16)
            xn[pl.ds(start, WIN)] = normed(rows, gain_fine[...])
            return 0

        lax.fori_loop(0, NW, gather, 0)
        for n in range(3):
            part = dot(xn[...], w_qkv_fine[:, n * D1 : (n + 1) * D1])
            if n == 0:
                part = part.astype(jnp.bfloat16) * jnp.bfloat16(HS**-0.5)
            qkv[:, n * D1 : (n + 1) * D1] = part.astype(jnp.bfloat16)
        odd = c % 2
        at_edge = lat == (1 - odd) * (n_lat - 1)
        which = jnp.where(at_edge, 1, 0)

        def window(w, _):
            rows = pl.ds(pl.multiple_of(w * WIN, 16), WIN)
            heads = []
            for pair in range(D1 // 128):
                lanes = [pl.ds(n * D1 + pair * 128, 128) for n in range(3)]
                heads.append(
                    attend_pair(
                        qkv[rows, lanes[0]],
                        qkv[rows, lanes[1]],
                        qkv[rows, lanes[2]],
                        bias_fine[which, 2 * pair],
                        bias_fine[which, 2 * pair + 1],
                    )
                )
            heads = jnp.concatenate(heads, axis=1)
            pieces[w] = dot(maps[FROM_WIN, w][:, :WIN], heads).astype(jnp.bfloat16)
            return 0

        lax.fori_loop(0, NW, window, 0)
        put_quarters(c, heads_send, heads_recv, IN_WINDOW)
        for k in range(1, 4):
            heads_copy(c, k).start()

    def merge(c):
        for k in range(1, 4):
            heads_copy(c, k).wait_recv()

        def regroup(w, _):
            rows = quart_rows(heads_recv, c, w, IN_TILE)
            pieces[w] = dot(maps[HEADS_GROUP, w], rows).astype(jnp.bfloat16)
            start = pl.multiple_of(w * NAT, 16)
            heads_nat[c, pl.ds(start, NAT)] = dot(maps[HEADS_NAT, w], rows).astype(jnp.bfloat16)
            return 0

        lax.fori_loop(0, NW, regroup, 0)
        pltpu.make_async_copy(heads_nat.at[c], heads_nat_hbm.at[c], out_sem.at[0, c]).start()
        for g in range(4):
            rows = assemble(lambda w: pieces[w, pl.ds(g * PIECE, PIECE)])
            group_heads[pl.ds(g * CROWS, CROWS)] = rows

        def regroup_tokens(w, _):
            pieces[w] = dot(maps[TO_GROUP, w], nat_rows(c, w)).astype(jnp.bfloat16)
            return 0

        lax.fori_loop(0, NW, regroup_tokens, 0)
        fine_rows[...] = dot(group_heads[...], w_out_fine[...])
        total = jnp.zeros((CROWS, 1), jnp.float32)
        for g in range(4):
            rows = pl.ds(g * CROWS, CROWS)
            own = assemble(lambda w: pieces[w, pl.ds(g * PIECE, PIECE)])
            values = fine_rows[rows] + own.astype(jnp.float32)
            fine_rows[rows] = values
            total = total + jnp.sum(values, axis=-1, keepdims=True)
        average = total / (4 * D1)
        total = jnp.zeros((CROWS, 1), jnp.float32)
        for g in range(4):
            centred = fine_rows[pl.ds(g * CROWS, CROWS)] - average
            total = total + jnp.sum(centred * centred, axis=-1, keepdims=True)
        inverse = lax.rsqrt(total / (4 * D1) + EPS)
        merged = jnp.zeros((CROWS, D2), jnp.float32)
        for g in range(4):
            lanes = pl.ds(g * D1, D1)
            centred = fine_rows[pl.ds(g * CROWS, CROWS)] - average
            part = (centred * inverse * gain_merge[:, lanes]).astype(jnp.bfloat16)
            merged = merged + dot(part, w_merge[lanes])
        coarse_in[c] = merged.astype(jnp.bfloat16)
        start = pl.multiple_of(member * STEP, STEP)
        coarse_recv[c, member] = coarse_in[c, pl.ds(start, PIECE)]
        for k in range(1, 4):
            coarse_copy(c, k).start()
        pltpu.make_async_copy(coarse_in.at[c], coarse_in_hbm.at[c], out_sem.at[1, c]).start()

    def coarse_attention(c):
        for k in range(1, 4):
            coarse_copy(c, k).wait_recv()
        rows = jnp.concatenate([coarse_recv[c, m] for m in range(4)], axis=0)
        values = dot(maps[TO_WIN, member][:WIN], rows)
        xn_coarse[...] = normed(values, gain_coarse[...])
        for n in range(3):
            lanes = pl.ds(n * D2, D2)
            part = dot(xn_coarse[...], w_qkv_coarse[:, lanes]).astype(jnp.bfloat16)
            if n == 0:
                part = part * jnp.bfloat16(HS**-0.5)
            qkv_coarse[:, lanes] = part
        heads = []
        for pair in range(D2 // 128):
            lanes = [pl.ds(n * D2 + pair * 128, 128) for n in range(3)]
            heads.append(
                attend_pair(
                    qkv_coarse[:, lanes[0]],
                    qkv_coarse[:, lanes[1]],
                    qkv_coarse[:, lanes[2]],
                    bias_coarse[2 * pair],
                    bias_coarse[2 * pair + 1],
                )
            )
        heads = jnp.concatenate(heads, axis=1)
        rows = dot(maps[FROM_WIN, member][:, :WIN], heads).astype(jnp.bfloat16)
        for m in range(4):
            back_send[c, m] = rows[m * PIECE : (m + 1) * PIECE]
        back_recv[c, member] = back_send[c, member]
        for k in range(1, 4):
            back_copy(c, k).start()

    def finish(c):
        for k in range(1, 4):
            back_copy(c, k).wait_recv()
        heads_coarse[c] = assemble(lambda w: back_recv[c, w])
        pltpu.make_async_copy(heads_coarse.at[c], heads_coarse_hbm.at[c], out_sem.at[2, c]).start()

    def step(s, _):
        for depth, stage in enumerate((fine_attention, merge, coarse_attention, finish)):

            @pl.when((s >= depth) & (s < n_chunks + depth))
            def _():
                stage(s - depth)

        return 0

    lax.fori_loop(0, n_chunks + 3, step, 0)

    def drain(c, _):
        for k in range(1, 4):
            fine_copy(c, k).wait_send()
            heads_copy(c, k).wait_send()
            coarse_copy(c, k).wait_send()
            back_copy(c, k).wait_send()
        pltpu.make_async_copy(heads_nat.at[c], heads_nat_hbm.at[c], out_sem.at[0, c]).wait()
        pltpu.make_async_copy(coarse_in.at[c], coarse_in_hbm.at[c], out_sem.at[1, c]).wait()
        pltpu.make_async_copy(heads_coarse.at[c], heads_coarse_hbm.at[c], out_sem.at[2, c]).wait()
        return 0

    lax.fori_loop(0, n_chunks, drain, 0)


def last_kernel(
    tokens, heads_nat, coarse_in, heads_coarse, w_out_fine, w_out_coarse, spread, fine_out, coarse_out
):
    fine = dot(heads_nat[0], w_out_fine[...]).reshape(2, 4, ROWS, 16, D1)
    fine_out[...] = fine[:, :, :, :COLS] + tokens[...].astype(jnp.float32)
    wide = dot(spread[...], jnp.concatenate([heads_coarse[0], coarse_in[0]], axis=1))
    coarse = dot(wide[:, :D2].astype(jnp.bfloat16), w_out_coarse[...]) + wide[:, D2:]
    coarse_out[...] = coarse.reshape(2, 4, HALF_R, 8, D2)[:, :, :, :HALF_C]


def body(
    fine_tokens,
    gain_fine,
    w_qkv_fine,
    bias_fine,
    w_out_fine,
    gain_merge,
    w_merge,
    gain_coarse,
    w_qkv_coarse,
    bias_coarse,
    w_out_coarse,
):
    batch = fine_tokens.shape[0]
    chunks = batch // 2
    bf16, f32 = jnp.bfloat16, jnp.float32
    maps = jnp.asarray(row_maps(), bf16)
    spread = jnp.asarray(spread_map(), bf16)
    hbm = pl.BlockSpec(memory_space=pl.ANY)
    vmem = pl.BlockSpec(memory_space=pltpu.VMEM)
    dma = pltpu.SemaphoreType.DMA
    heads_nat, coarse_in, heads_coarse = pl.pallas_call(
        functools.partial(main_kernel, chunks, lax.axis_size("lat"), lax.axis_size("lon")),
        out_shape=(
            jax.ShapeDtypeStruct((chunks, NW * NAT, D1), bf16),
            jax.ShapeDtypeStruct((chunks, CROWS, D2), bf16),
            jax.ShapeDtypeStruct((chunks, CROWS, D2), bf16),
        ),
        in_specs=[hbm, vmem, hbm, hbm, hbm, vmem, hbm, vmem, hbm, hbm, hbm],
        out_specs=(hbm, hbm, hbm),
        scratch_shapes=[
            pltpu.VMEM((chunks, 2, 4, ROWS, COLS, D1), bf16),
            pltpu.VMEM(w_qkv_fine.shape, bf16),
            pltpu.VMEM((2,) + bias_fine.shape, f32),
            pltpu.VMEM(w_out_fine.shape, bf16),
            pltpu.VMEM(w_merge.shape, bf16),
            pltpu.VMEM(w_qkv_coarse.shape, bf16),
            pltpu.VMEM(bias_coarse.shape, f32),
            pltpu.VMEM(maps.shape, bf16),
            pltpu.VMEM((chunks, 2 * 4 * ROWS, 16, D1), bf16),
            pltpu.VMEM((NW, 4 * PIECE, D1), bf16),
            pltpu.VMEM((chunks, 4, CROWS, D1), bf16),
            pltpu.VMEM((chunks, 4, CROWS, D1), bf16),
            pltpu.VMEM((NW * WIN, D1), bf16),
            pltpu.VMEM((NW * WIN, 3 * D1), bf16),
            pltpu.VMEM((chunks, 4, CROWS, D1), bf16),
            pltpu.VMEM((chunks, 4, CROWS, D1), bf16),
            pltpu.VMEM((4 * CROWS, D1), bf16),
            pltpu.VMEM((4 * CROWS, D1), f32),
            pltpu.VMEM((chunks, NW * NAT, D1), bf16),
            pltpu.VMEM((chunks, CROWS, D2), bf16),
            pltpu.VMEM((chunks, 4, PIECE, D2), bf16),
            pltpu.VMEM((WIN, D2), bf16),
            pltpu.VMEM((WIN, 3 * D2), bf16),
            pltpu.VMEM((chunks, 4, PIECE, D2), bf16),
            pltpu.VMEM((chunks, 4, PIECE, D2), bf16),
            pltpu.VMEM((chunks, CROWS, D2), bf16),
            dma((7,)),
            dma((chunks,)),
        ]
        + [dma((chunks, 4)) for _ in range(8)]
        + [dma((3, chunks))],
        compiler_params=pltpu.CompilerParams(
            collective_id=0, has_side_effects=True, vmem_limit_bytes=VMEM_LIMIT
        ),
        name="window_levels",
    )(
        fine_tokens,
        gain_fine[None],
        w_qkv_fine,
        bias_fine,
        w_out_fine,
        gain_merge[None],
        w_merge,
        gain_coarse[None],
        w_qkv_coarse,
        bias_coarse,
        maps,
    )
    chunk3 = lambda c: (c, 0, 0)
    chunk5 = lambda c: (c, 0, 0, 0, 0)
    whole = lambda c: (0, 0)
    return pl.pallas_call(
        last_kernel,
        grid=(chunks,),
        out_shape=(
            jax.ShapeDtypeStruct(fine_tokens.shape, f32),
            jax.ShapeDtypeStruct((batch, 4, HALF_R, HALF_C, D2), f32),
        ),
        in_specs=[
            pl.BlockSpec((2, 4, ROWS, COLS, D1), chunk5),
            pl.BlockSpec((1, NW * NAT, D1), chunk3),
            pl.BlockSpec((1, CROWS, D2), chunk3),
            pl.BlockSpec((1, CROWS, D2), chunk3),
            pl.BlockSpec((D1, D1), whole),
            pl.BlockSpec((D2, D2), whole),
            pl.BlockSpec(spread.shape, whole),
        ],
        out_specs=(
            pl.BlockSpec((2, 4, ROWS, COLS, D1), chunk5),
            pl.BlockSpec((2, 4, HALF_R, HALF_C, D2), chunk5),
        ),
        compiler_params=pltpu.CompilerParams(vmem_limit_bytes=VMEM_LIMIT),
        name="last_projections",
    )(fine_tokens, heads_nat, coarse_in, heads_coarse, w_out_fine, w_out_coarse, spread)


def solution(mesh):
    tile = P(None, None, "lat", "lon", None)
    return jax.shard_map(
        body,
        mesh=mesh,
        in_specs=(tile,) + (P(),) * 10,
        out_specs=(tile, tile),
        check_vma=False,
    )
```

profile of v0, /device:TPU:42, one launch (start us, length us, event | category | flops | bytes accessed | tf_op | source)
XLA Modules:
  0.0 127.8 jit_solution(15496229900589974885)
XLA Ops:
  0.6 4.1 %copy.16.tokens_hbm.tokens = bf16[8,4,6,12,512]{4,3,2,1,0:T(8,128)(2,1)} copy(bf16[8,4,6,12,512]{4,1,3,2,0:T(4,128)(2,1)} %param.13) | data formatting | bytes 4718592 | tf_op args[0]
  4.7 100.4 %window_levels.1 = (bf16[4,768,512]{2,1,0:T(8,128)(2,1)}, bf16[4,144,1024]{2,1,0:T(8,128)(2,1)}, bf16[4,144,1024]{2,1,0:T(8,128)(2,1)}) custom-call(bf16[8,4,6,12,512]{4,3,2,1,0:T(8,128)(2,1)} %copy.16.tokens_hbm.tokens, f32[1,512]{1,0:T(1,128)} %bitcast.5, bf16[512,1536]{1,0:T(8,128)(2,1)} %w_qkv_fine_hbm.1, f32[8,144,144]{2,1,0:T(8,128)} %bias_fine_hbm.1, ...), custom_call_target="tpu_custom_call" | custom-call | tf_op jit(solution)/shard_map/window_levels/pallas_call | solution.py:495
  105.1 10.0 %last_projections.1 = (f32[8,4,6,12,512]{4,3,2,1,0:T(8,128)}, f32[8,4,3,6,1024]{4,3,2,1,0:T(8,128)}) custom-call(bf16[8,4,6,12,512]{4,3,2,1,0:T(8,128)(2,1)} %copy.16.tokens_hbm.tokens, bf16[4,768,512]{2,1,0:T(8,128)(2,1)} %get-tuple-element.5.heads_nat, bf16[4,144,1024]{2,1,0:T(8,128)(2,1)} %get-tuple-element.6.coarse_in, ...), custom_call_target="tpu_custom_call" | custom-call | tf_op jit(solution)/shard_map/last_projections/pallas_call | solution.py:556
  115.0 0.0 copy-start
  115.0 9.5 %copy.17 = f32[8,4,6,12,512]{4,1,3,2,0:T(4,128)} copy(f32[8,4,6,12,512]{4,3,2,1,0:T(8,128)} %get-tuple-element.8) | data formatting | bytes 9437184 | tf_op jit(solution)/shard_map/last_projections/pallas_call | solution.py:556
  124.5 0.0 copy-done
  124.5 3.3 %copy.18 = f32[8,4,3,6,1024]{4,1,3,2,0:T(4,128)} copy(f32[8,4,3,6,1024]{4,3,2,1,0:T(8,128)S(1)} %copy-done) | data formatting | bytes 4718592 | tf_op jit(solution)/shard_map/last_projections/pallas_call | solution.py:556
Async XLA Ops:
  115.0 9.5 %copy-start = (f32[8,4,3,6,1024]{4,3,2,1,0:T(8,128)S(1)}, f32[8,4,3,6,1024]{4,3,2,1,0:T(8,128)}, u32[]{:S(2)}) copy-start(f32[8,4,3,6,1024]{4,3,2,1,0:T(8,128)} %get-tuple-element.9) | copy-start | bytes 7077892
where the time goes:
time: 129 us; the launch traced here: 128 us
  Pallas kernels  110 us (85%)
  local copies, waits for them, and re-layouts  16.8 us (13%)
    pallas_call x1, Pallas kernels, body(): pl.pallas_call(functools.partial(main_kernel, chunks, lax.axis_size('lat'...  100 us
    pallas_call x2, local copies, waits for them, and re-layouts, body(): pl.pallas_call(last_kernel, grid=(chunks,), out_shape=(jax.ShapeDtypeStru...  12.8 us
    pallas_call x1, Pallas kernels, body(): pl.pallas_call(last_kernel, grid=(chunks,), out_shape=(jax.ShapeDtypeStru...  9.95 us
    unnamed x3, local copies, waits for them, and re-layouts  4.06 us

commit v1 on v0

v1 whole, which is shorter than its diff:
```python
import functools

import jax
import jax.numpy as jnp
import numpy as np
from jax import lax
from jax.experimental import pallas as pl
from jax.experimental.pallas import tpu as pltpu
from jax.sharding import PartitionSpec as P

EPS = 1e-05
NEG = -1e30
ROWS, COLS, LEVELS, WLEV, HS = 6, 12, 4, 2, 64
HALF_R, HALF_C = ROWS // 2, COLS // 2
WIN = WLEV * ROWS * COLS
PAIR = 2 * WIN
NW = 4
CROWS = 2 * HALF_R * HALF_C * LEVELS
D1, D2 = 512, 1024
TO_SEND, TO_WIN, FROM_WIN = range(3)
MESH = pl.DeviceIdType.MESH
VMEM_LIMIT = 58 * 1024 * 1024


def pair_maps():
    to_win = np.zeros((PAIR, PAIR), np.float32)
    for lev in range(LEVELS):
        for r in range(ROWS):
            for c in range(COLS):
                q = (1 - r // HALF_R) * 2 + 1 - c // HALF_C
                src = ((q * HALF_R + r % HALF_R) * HALF_C + c % HALF_C) * LEVELS + lev
                win = lev // WLEV * WIN + (lev % WLEV * ROWS + r) * COLS + c
                to_win[win, src] = 1
    return np.stack([to_win, to_win.T])


def coarse_maps():
    to_send = np.zeros((CROWS, CROWS), np.float32)
    to_win = np.zeros((CROWS, CROWS), np.float32)
    part = CROWS // NW
    for b in range(2):
        for r in range(HALF_R):
            for c in range(HALF_C):
                for lev in range(LEVELS):
                    nat = ((b * HALF_R + r) * HALF_C + c) * LEVELS + lev
                    t = (lev % WLEV * HALF_R + r) * HALF_C + c
                    to_send[(b * 2 + lev // WLEV) * part + t, nat] = 1
    for lev in range(WLEV):
        for r in range(ROWS):
            for c in range(COLS):
                m = r // HALF_R * 2 + c // HALF_C
                t = (lev * HALF_R + r % HALF_R) * HALF_C + c % HALF_C
                to_win[(lev * ROWS + r) * COLS + c, m * part + t] = 1
    return np.stack([to_send, to_win, to_win.T])


def dot(a, b):
    return jnp.dot(a, b, preferred_element_type=jnp.float32)


def dot_t(a, b):
    return lax.dot_general(a, b, (((1,), (1,)), ((), ())), preferred_element_type=jnp.float32)


def normed(values, gain):
    average = jnp.mean(values, axis=-1, keepdims=True)
    centred = values - average
    variance = jnp.mean(centred * centred, axis=-1, keepdims=True)
    return (centred * lax.rsqrt(variance + EPS) * gain).astype(jnp.bfloat16)


def attend_pair(query, key, value, bias0, bias1):
    low = lax.broadcasted_iota(jnp.int32, (WIN, 128), 1) < HS
    one = jnp.ones((), jnp.bfloat16)
    zero = jnp.zeros((), jnp.bfloat16)
    results = []
    for side, bias in ((low, bias0), (jnp.logical_not(low), bias1)):
        scores = dot_t(jnp.where(side, query, zero), key) + bias
        top = jnp.max(scores, axis=-1, keepdims=True)
        probs = jnp.exp(scores - top).astype(jnp.bfloat16)
        results.append(dot(probs, jnp.where(side, value, one)))
    total = jnp.where(low, results[0], results[1])
    weight = pltpu.roll(jnp.where(low, results[1], results[0]), HS, 1)
    return (total / weight).astype(jnp.bfloat16)


def main_kernel(
    n_chunks,
    n_lat,
    n_lon,
    tokens_hbm,
    gain_fine,
    w_qkv_fine_hbm,
    bias_fine_hbm,
    w_out_fine_hbm,
    gain_merge,
    w_merge_hbm,
    gain_coarse,
    w_qkv_coarse_hbm,
    bias_coarse_hbm,
    maps_hbm,
    coarse_maps_hbm,
    heads_hbm,
    coarse_in_hbm,
    heads_coarse_hbm,
    tokens,
    w_qkv_fine,
    bias_fine,
    w_out_fine,
    w_merge,
    w_qkv_coarse,
    bias_coarse,
    maps,
    cmaps,
    fine_recv,
    xn,
    qkv,
    win_heads,
    heads_send,
    heads,
    fine_rows,
    merged,
    coarse_in,
    coarse_send,
    coarse_recv,
    xn_coarse,
    qkv_coarse,
    back_send,
    back_recv,
    load_sem,
    token_sem,
    own_sem,
    fine_ssem,
    fine_rsem,
    heads_ssem,
    heads_rsem,
    coarse_ssem,
    coarse_rsem,
    back_ssem,
    back_rsem,
    out_sem,
):
    lat = lax.axis_index("lat")
    lon = lax.axis_index("lon")
    member = (lat % 2) * 2 + lon % 2

    def at(dlat, dlon):
        return (lax.rem(lat + dlat + n_lat, n_lat), lax.rem(lon + dlon + n_lon, n_lon))

    def partner(k):
        return (
            lat + (k // 2) * (1 - 2 * (lat % 2)),
            lon + (k % 2) * (1 - 2 * (lon % 2)),
        )

    def way(c):
        return 2 * (c % 2) - 1

    def quarter(c, k):
        return 3 - k + (c % 2) * (2 * k - 3)

    def tile_part(ref, c, q):
        return ref.at[
            pl.ds(2 * c, 2), pl.ds(q // 2 * HALF_R, HALF_R), pl.ds(q % 2 * HALF_C, HALF_C)
        ]

    def fine_copy(c, k):
        q = quarter(c, k)
        return pltpu.make_async_remote_copy(
            tile_part(tokens_hbm, c, q),
            fine_recv.at[c, q],
            fine_ssem.at[c, k],
            fine_rsem.at[c, k],
            device_id=at(k // 2 * way(c), k % 2 * way(c)),
            device_id_type=MESH,
        )

    def own_copy(c):
        q = quarter(c, 0)
        return pltpu.make_async_copy(
            tile_part(tokens_hbm, c, q), fine_recv.at[c, q], own_sem.at[c]
        )

    def heads_copy(c, k):
        q = quarter(c, k)
        return pltpu.make_async_remote_copy(
            heads_send.at[c, q],
            tile_part(heads, c, q),
            heads_ssem.at[c, k],
            heads_rsem.at[c, k],
            device_id=at(-(k // 2) * way(c), -(k % 2) * way(c)),
            device_id_type=MESH,
        )

    def other(k):
        mine_lat, mine_lon = lat % 2, lon % 2
        to_lat = mine_lat + (k // 2) * (1 - 2 * mine_lat)
        to_lon = mine_lon + (k % 2) * (1 - 2 * mine_lon)
        return to_lat * 2 + to_lon

    def group_copy(c, k, send, recv, ssem, rsem):
        return pltpu.make_async_remote_copy(
            send.at[c, other(k)],
            recv.at[c, member],
            ssem.at[c, k],
            rsem.at[c, k],
            device_id=partner(k),
            device_id_type=MESH,
        )

    def coarse_copy(c, k):
        return group_copy(c, k, coarse_send, coarse_recv, coarse_ssem, coarse_rsem)

    def back_copy(c, k):
        return group_copy(c, k, back_send, back_recv, back_ssem, back_rsem)

    def token_copy(c):
        part = pl.ds(2 * c, 2)
        return pltpu.make_async_copy(tokens_hbm.at[part], tokens.at[part], token_sem.at[c])

    def result_copy(n, c):
        part = pl.ds(2 * c, 2)
        src, dst = (
            (heads.at[part], heads_hbm.at[part]),
            (coarse_in.at[c], coarse_in_hbm.at[c]),
            (back_recv.at[c], heads_coarse_hbm.at[c]),
        )[n]
        return pltpu.make_async_copy(src, dst, out_sem.at[n, c])

    def load(n, src, dst):
        return pltpu.make_async_copy(src, dst, load_sem.at[n])

    loads = [
        load(0, maps_hbm, maps),
        load(1, w_qkv_fine_hbm, w_qkv_fine),
        load(2, bias_fine_hbm, bias_fine.at[0]),
        load(3, w_out_fine_hbm, w_out_fine),
        load(4, w_merge_hbm, w_merge),
        load(5, coarse_maps_hbm, cmaps),
        load(6, w_qkv_coarse_hbm, w_qkv_coarse),
        load(7, bias_coarse_hbm, bias_coarse),
    ]

    barrier = pltpu.get_barrier_semaphore()
    for near in (at(0, -1), at(0, 1), at(-1, 0), at(1, 0), at(-1, -1), at(1, 1), partner(3)):
        pl.semaphore_signal(barrier, inc=1, device_id=near, device_id_type=MESH)
    pl.semaphore_wait(barrier, 7)

    def send_tokens(c, _):
        for k in (3, 2, 1):
            fine_copy(c, k).start()
        own_copy(c).start()
        return 0

    lax.fori_loop(0, n_chunks, send_tokens, 0)
    for copy in loads[:3]:
        copy.start()
    for c in range(n_chunks):
        token_copy(c).start()
    for copy in loads[3:]:
        copy.start()

    loads[2].wait()
    token_q = lax.broadcasted_iota(jnp.int32, (WIN, WIN), 0)
    token_k = lax.broadcasted_iota(jnp.int32, (WIN, WIN), 1)
    late_q = (token_q % (ROWS * COLS)) >= HALF_R * COLS
    late_k = (token_k % (ROWS * COLS)) >= HALF_R * COLS
    mask = jnp.where(late_q == late_k, 0.0, NEG)
    for h in range(D1 // HS):
        bias_fine[1, h] = bias_fine[0, h] + mask
    loads[0].wait()
    loads[1].wait()

    def fine_attention(c):
        own_copy(c).wait()
        for k in (1, 2, 3):
            fine_copy(c, k).wait_recv()
        for b in range(2):
            rows = fine_recv[c, :, b].reshape(PAIR, D1)
            xn[pl.ds(b * PAIR, PAIR)] = normed(dot(maps[0], rows), gain_fine[...])
        for n in range(3):
            part = dot(xn[...], w_qkv_fine[:, n * D1 : (n + 1) * D1]).astype(jnp.bfloat16)
            if n == 0:
                part = part * jnp.bfloat16(HS**-0.5)
            qkv[:, n * D1 : (n + 1) * D1] = part
        at_edge = lat == (1 - c % 2) * (n_lat - 1)
        which = jnp.where(at_edge, 1, 0)

        def window(w, _):
            rows = pl.ds(pl.multiple_of(w * WIN, 16), WIN)
            for pair in range(D1 // 128):
                lanes = [pl.ds(n * D1 + pair * 128, 128) for n in range(3)]
                win_heads[rows, lanes[0]] = attend_pair(
                    qkv[rows, lanes[0]],
                    qkv[rows, lanes[1]],
                    qkv[rows, lanes[2]],
                    bias_fine[which, 2 * pair],
                    bias_fine[which, 2 * pair + 1],
                )
            return 0

        lax.fori_loop(0, NW, window, 0)
        for b in range(2):
            rows = dot(maps[1], win_heads[pl.ds(b * PAIR, PAIR)]).astype(jnp.bfloat16)
            heads_send[c, :, b] = rows.reshape(4, HALF_R, HALF_C, LEVELS, D1)
        for k in (3, 2, 1):
            heads_copy(c, k).start()
        own = quarter(c, 0)
        tile_part(heads, c, own)[...] = heads_send[c, own]

    def merge(c):
        @pl.when(c == 0)
        def _():
            loads[3].wait()
            loads[4].wait()
            loads[5].wait()

        token_copy(c).wait()
        for k in (1, 2, 3):
            heads_copy(c, k).wait_recv()
        result_copy(0, c).start()
        part = pl.ds(2 * c, 2)
        rows = dot(heads[part].reshape(4 * CROWS, D1), w_out_fine[...])
        rows = rows + tokens[part].reshape(4 * CROWS, D1).astype(jnp.float32)
        fine_rows[...] = rows.reshape(2, HALF_R, 2, HALF_C, 2, LEVELS, D1)
        total = jnp.zeros((CROWS, 1), jnp.float32)
        for g in range(4):
            values = fine_rows[:, :, g % 2, :, g // 2].reshape(CROWS, D1)
            total = total + jnp.sum(values, axis=-1, keepdims=True)
        average = total / (4 * D1)
        total = jnp.zeros((CROWS, 1), jnp.float32)
        for g in range(4):
            centred = fine_rows[:, :, g % 2, :, g // 2].reshape(CROWS, D1) - average
            total = total + jnp.sum(centred * centred, axis=-1, keepdims=True)
        inverse = lax.rsqrt(total / (4 * D1) + EPS)
        for g in range(4):
            lanes = pl.ds(g * D1, D1)
            centred = fine_rows[:, :, g % 2, :, g // 2].reshape(CROWS, D1) - average
            merged[:, lanes] = (centred * inverse * gain_merge[:, lanes]).astype(jnp.bfloat16)
        coarse = dot(merged[...], w_merge[...]).astype(jnp.bfloat16)
        coarse_in[c] = coarse
        rows = dot(cmaps[TO_SEND], coarse).astype(jnp.bfloat16)
        coarse_send[c] = rows.reshape(coarse_send.shape[1:])
        for k in (3, 2, 1):
            coarse_copy(c, k).start()
        coarse_recv[c, member] = coarse_send[c, member]
        result_copy(1, c).start()

    def coarse_attention(c):
        @pl.when(c == 0)
        def _():
            loads[6].wait()
            loads[7].wait()

        for k in (1, 2, 3):
            coarse_copy(c, k).wait_recv()
        values = dot(cmaps[TO_WIN], coarse_recv[c].reshape(WIN, D2))
        xn_coarse[...] = normed(values, gain_coarse[...])
        for n in range(3):
            lanes = pl.ds(n * D2, D2)
            part = dot(xn_coarse[...], w_qkv_coarse[:, lanes]).astype(jnp.bfloat16)
            if n == 0:
                part = part * jnp.bfloat16(HS**-0.5)
            qkv_coarse[:, lanes] = part
        results = []
        for pair in range(D2 // 128):
            lanes = [pl.ds(n * D2 + pair * 128, 128) for n in range(3)]
            results.append(
                attend_pair(
                    qkv_coarse[:, lanes[0]],
                    qkv_coarse[:, lanes[1]],
                    qkv_coarse[:, lanes[2]],
                    bias_coarse[2 * pair],
                    bias_coarse[2 * pair + 1],
                )
            )
        rows = dot(cmaps[FROM_WIN], jnp.concatenate(results, axis=1)).astype(jnp.bfloat16)
        back_send[c] = rows.reshape(back_send.shape[1:])
        for k in (3, 2, 1):
            back_copy(c, k).start()
        back_recv[c, member] = back_send[c, member]

    def finish(c):
        for k in (1, 2, 3):
            back_copy(c, k).wait_recv()
        result_copy(2, c).start()

    def step(s, _):
        for depth, stage in enumerate((fine_attention, merge, coarse_attention, finish)):

            @pl.when((s >= depth) & (s < n_chunks + depth))
            def _():
                stage(s - depth)

        return 0

    lax.fori_loop(0, n_chunks + 3, step, 0)

    def drain(c, _):
        for k in (1, 2, 3):
            fine_copy(c, k).wait_send()
            heads_copy(c, k).wait_send()
            coarse_copy(c, k).wait_send()
            back_copy(c, k).wait_send()
        for n in range(3):
            result_copy(n, c).wait()
        return 0

    lax.fori_loop(0, n_chunks, drain, 0)


def last_kernel(
    tokens, heads, coarse_in, heads_coarse, w_out_fine, w_out_coarse, maps, fine_out, coarse_out
):
    fine = dot(heads[...].reshape(4 * CROWS, D1), w_out_fine[...])
    fine = fine + tokens[...].reshape(4 * CROWS, D1).astype(jnp.float32)
    fine_out[...] = fine.reshape(fine_out.shape)
    rows = dot(maps[...], heads_coarse[...].reshape(CROWS, D2)).astype(jnp.bfloat16)
    coarse = dot(rows, w_out_coarse[...]) + coarse_in[0].astype(jnp.float32)
    coarse_out[...] = coarse.reshape(coarse_out.shape)


def body(
    fine_tokens,
    gain_fine,
    w_qkv_fine,
    bias_fine,
    w_out_fine,
    gain_merge,
    w_merge,
    gain_coarse,
    w_qkv_coarse,
    bias_coarse,
    w_out_coarse,
):
    tokens = fine_tokens.transpose(0, 2, 3, 1, 4)
    batch = tokens.shape[0]
    chunks = batch // 2
    bf16, f32 = jnp.bfloat16, jnp.float32
    maps = jnp.asarray(pair_maps(), bf16)
    cmaps = jnp.asarray(coarse_maps(), bf16)
    cmap_back = jnp.asarray(coarse_maps()[TO_SEND].T, bf16)
    hbm = pl.BlockSpec(memory_space=pl.ANY)
    vmem = pl.BlockSpec(memory_space=pltpu.VMEM)
    dma = pltpu.SemaphoreType.DMA
    slots = (chunks, NW, CROWS // NW // 4, 4, D2)
    heads, coarse_in, heads_coarse = pl.pallas_call(
        functools.partial(main_kernel, chunks, lax.axis_size("lat"), lax.axis_size("lon")),
        out_shape=(
            jax.ShapeDtypeStruct(tokens.shape, bf16),
            jax.ShapeDtypeStruct((chunks, CROWS, D2), bf16),
            jax.ShapeDtypeStruct(slots, bf16),
        ),
        in_specs=[hbm, vmem, hbm, hbm, hbm, vmem, hbm, vmem, hbm, hbm, hbm, hbm],
        out_specs=(hbm, hbm, hbm),
        scratch_shapes=[
            pltpu.VMEM(tokens.shape, bf16),
            pltpu.VMEM(w_qkv_fine.shape, bf16),
            pltpu.VMEM((2,) + bias_fine.shape, f32),
            pltpu.VMEM(w_out_fine.shape, bf16),
            pltpu.VMEM(w_merge.shape, bf16),
            pltpu.VMEM(w_qkv_coarse.shape, bf16),
            pltpu.VMEM(bias_coarse.shape, f32),
            pltpu.VMEM(maps.shape, bf16),
            pltpu.VMEM(cmaps.shape, bf16),
            pltpu.VMEM((chunks, 4, 2, HALF_R, HALF_C, LEVELS, D1), bf16),
            pltpu.VMEM((NW * WIN, D1), bf16),
            pltpu.VMEM((NW * WIN, 3 * D1), bf16),
            pltpu.VMEM((NW * WIN, D1), bf16),
            pltpu.VMEM((chunks, 4, 2, HALF_R, HALF_C, LEVELS, D1), bf16),
            pltpu.VMEM(tokens.shape, bf16),
            pltpu.VMEM((2, HALF_R, 2, HALF_C, 2, LEVELS, D1), f32),
            pltpu.VMEM((CROWS, 4 * D1), bf16),
            pltpu.VMEM((chunks, CROWS, D2), bf16),
            pltpu.VMEM(slots, bf16),
            pltpu.VMEM(slots, bf16),
            pltpu.VMEM((WIN, D2), bf16),
            pltpu.VMEM((WIN, 3 * D2), bf16),
            pltpu.VMEM(slots, bf16),
            pltpu.VMEM(slots, bf16),
            dma((8,)),
            dma((chunks,)),
            dma((chunks,)),
        ]
        + [dma((chunks, 4)) for _ in range(8)]
        + [dma((3, chunks))],
        compiler_params=pltpu.CompilerParams(
            collective_id=0, has_side_effects=True, vmem_limit_bytes=VMEM_LIMIT
        ),
        name="window_levels",
    )(
        tokens,
        gain_fine[None],
        w_qkv_fine,
        bias_fine,
        w_out_fine,
        gain_merge[None],
        w_merge,
        gain_coarse[None],
        w_qkv_coarse,
        bias_coarse,
        maps,
        cmaps,
    )
    chunk3 = lambda c: (c, 0, 0)
    chunk5 = lambda c: (c, 0, 0, 0, 0)
    whole = lambda c: (0, 0)
    fine_out, coarse_out = pl.pallas_call(
        last_kernel,
        grid=(chunks,),
        out_shape=(
            jax.ShapeDtypeStruct(tokens.shape, f32),
            jax.ShapeDtypeStruct((batch, HALF_R, HALF_C, LEVELS, D2), f32),
        ),
        in_specs=[
            pl.BlockSpec((2, ROWS, COLS, LEVELS, D1), chunk5),
            pl.BlockSpec((2, ROWS, COLS, LEVELS, D1), chunk5),
            pl.BlockSpec((1, CROWS, D2), chunk3),
            pl.BlockSpec((1,) + slots[1:], chunk5),
            pl.BlockSpec((D1, D1), whole),
            pl.BlockSpec((D2, D2), whole),
            pl.BlockSpec(cmap_back.shape, whole),
        ],
        out_specs=(
            pl.BlockSpec((2, ROWS, COLS, LEVELS, D1), chunk5),
            pl.BlockSpec((2, HALF_R, HALF_C, LEVELS, D2), chunk5),
        ),
        compiler_params=pltpu.CompilerParams(vmem_limit_bytes=VMEM_LIMIT),
        name="last_projections",
    )(tokens, heads, coarse_in, heads_coarse, w_out_fine, w_out_coarse, cmap_back)
    return fine_out.transpose(0, 3, 1, 2, 4), coarse_out.transpose(0, 3, 1, 2, 4)


def solution(mesh):
    tile = P(None, None, "lat", "lon", None)
    return jax.shard_map(
        body,
        mesh=mesh,
        in_specs=(tile,) + (P(),) * 10,
        out_specs=(tile, tile),
        check_vma=False,
    )
```

time: 129 us -> 94 us (0.73)
  the two profiles are of different devices: /device:TPU:42 before, /device:TPU:52 now
where the time goes in v1:
time: 94 us; the launch traced here: 93.8 us
  Pallas kernels  93.2 us (99%)
    pallas_call x1, Pallas kernels, body(): pl.pallas_call(functools.partial(main_kernel, chunks, lax.axis_size('lat'...  84.9 us
    pallas_call x1, Pallas kernels, body(): pl.pallas_call(last_kernel, grid=(chunks,), out_shape=(jax.ShapeDtypeStru...  8.31 us

profile of v1, /device:TPU:52, one launch (start us, length us, event | category | flops | bytes accessed | tf_op | source)
XLA Modules:
  0.0 93.8 jit_solution(1448997985712684107)
XLA Ops:
  0.6 84.9 %window_levels.1 = (bf16[8,6,12,4,512]{4,3,2,1,0:T(4,128)(2,1)}, bf16[4,144,1024]{2,1,0:T(8,128)(2,1)}, bf16[4,4,9,4,1024]{4,3,2,1,0:T(4,128)(2,1)}) custom-call(bf16[8,6,12,4,512]{4,3,2,1,0:T(4,128)(2,1)} %bitcast.6, f32[1,512]{1,0:T(1,128)} %bitcast.10, bf16[512,1536]{1,0:T(8,128)(2,1)} %w_qkv_fine_hbm.1, f32[8,144,144]{2,1,0:T(8,128)} %bias_fine_hbm.1, ...), custom_call_target="tpu_custom_call" | custom-call | tf_op jit(solution)/shard_map/window_levels/pallas_call | solution.py:447
  85.5 8.3 %last_projections.1 = (f32[8,6,12,4,512]{4,3,2,1,0:T(4,128)}, f32[8,3,6,4,1024]{4,3,2,1,0:T(4,128)}) custom-call(bf16[8,6,12,4,512]{4,3,2,1,0:T(4,128)(2,1)} %bitcast.7, bf16[8,6,12,4,512]{4,3,2,1,0:T(4,128)(2,1)} %get-tuple-element.7.heads, bf16[4,144,1024]{2,1,0:T(8,128)(2,1)} %get-tuple-element.8.coarse_in, ...), custom_call_target="tpu_custom_call" | custom-call | tf_op jit(solution)/shard_map/last_projections/pallas_call | solution.py:508

commit v2 on v1

--- a/solution.py
+++ b/solution.py
@@ -15,11 +15,12 @@
 WIN = WLEV * ROWS * COLS
 PAIR = 2 * WIN
 NW = 4
+AHEAD = 2
 CROWS = 2 * HALF_R * HALF_C * LEVELS
 D1, D2 = 512, 1024
-TO_SEND, TO_WIN, FROM_WIN = range(3)
+TO_SEND, TO_WIN, FROM_WIN, FROM_SEND = range(4)
 MESH = pl.DeviceIdType.MESH
-VMEM_LIMIT = 58 * 1024 * 1024
+VMEM_LIMIT = 52 * 1024 * 1024
 
 
 def pair_maps():
@@ -51,7 +52,7 @@
                 m = r // HALF_R * 2 + c // HALF_C
                 t = (lev * HALF_R + r % HALF_R) * HALF_C + c % HALF_C
                 to_win[(lev * ROWS + r) * COLS + c, m * part + t] = 1
-    return np.stack([to_send, to_win, to_win.T])
+    return np.stack([to_send, to_win, to_win.T, to_send.T])
 
 
 def dot(a, b):
@@ -100,9 +101,9 @@
     bias_coarse_hbm,
     maps_hbm,
     coarse_maps_hbm,
-    heads_hbm,
-    coarse_in_hbm,
-    heads_coarse_hbm,
+    w_out_coarse_hbm,
+    fine_out,
+    coarse_out,
     tokens,
     w_qkv_fine,
     bias_fine,
@@ -110,6 +111,7 @@
     w_merge,
     w_qkv_coarse,
     bias_coarse,
+    w_out_coarse,
     maps,
     cmaps,
     fine_recv,
@@ -118,7 +120,6 @@
     win_heads,
     heads_send,
     heads,
-    fine_rows,
     merged,
     coarse_in,
     coarse_send,
@@ -138,7 +139,6 @@
     coarse_rsem,
     back_ssem,
     back_rsem,
-    out_sem,
 ):
     lat = lax.axis_index("lat")
     lon = lax.axis_index("lon")
@@ -218,15 +218,6 @@
         part = pl.ds(2 * c, 2)
         return pltpu.make_async_copy(tokens_hbm.at[part], tokens.at[part], token_sem.at[c])
 
-    def result_copy(n, c):
-        part = pl.ds(2 * c, 2)
-        src, dst = (
-            (heads.at[part], heads_hbm.at[part]),
-            (coarse_in.at[c], coarse_in_hbm.at[c]),
-            (back_recv.at[c], heads_coarse_hbm.at[c]),
-        )[n]
-        return pltpu.make_async_copy(src, dst, out_sem.at[n, c])
-
     def load(n, src, dst):
         return pltpu.make_async_copy(src, dst, load_sem.at[n])
 
@@ -239,6 +230,7 @@
         load(5, coarse_maps_hbm, cmaps),
         load(6, w_qkv_coarse_hbm, w_qkv_coarse),
         load(7, bias_coarse_hbm, bias_coarse),
+        load(8, w_out_coarse_hbm, w_out_coarse),
     ]
 
     barrier = pltpu.get_barrier_semaphore()
@@ -252,7 +244,7 @@
         own_copy(c).start()
         return 0
 
-    lax.fori_loop(0, n_chunks, send_tokens, 0)
+    lax.fori_loop(0, AHEAD, send_tokens, 0)
     for copy in loads[:3]:
         copy.start()
     for c in range(n_chunks):
@@ -275,6 +267,11 @@
         own_copy(c).wait()
         for k in (1, 2, 3):
             fine_copy(c, k).wait_recv()
+
+        @pl.when(c + AHEAD < n_chunks)
+        def _():
+            send_tokens(c + AHEAD, 0)
+
         for b in range(2):
             rows = fine_recv[c, :, b].reshape(PAIR, D1)
             xn[pl.ds(b * PAIR, PAIR)] = normed(dot(maps[0], rows), gain_fine[...])
@@ -318,24 +315,23 @@
         token_copy(c).wait()
         for k in (1, 2, 3):
             heads_copy(c, k).wait_recv()
-        result_copy(0, c).start()
         part = pl.ds(2 * c, 2)
         rows = dot(heads[part].reshape(4 * CROWS, D1), w_out_fine[...])
         rows = rows + tokens[part].reshape(4 * CROWS, D1).astype(jnp.float32)
-        fine_rows[...] = rows.reshape(2, HALF_R, 2, HALF_C, 2, LEVELS, D1)
+        fine_out[part] = rows.reshape(2, HALF_R, 2, HALF_C, 2, LEVELS, D1)
         total = jnp.zeros((CROWS, 1), jnp.float32)
         for g in range(4):
-            values = fine_rows[:, :, g % 2, :, g // 2].reshape(CROWS, D1)
+            values = fine_out[part, :, g % 2, :, g // 2].reshape(CROWS, D1)
             total = total + jnp.sum(values, axis=-1, keepdims=True)
         average = total / (4 * D1)
         total = jnp.zeros((CROWS, 1), jnp.float32)
         for g in range(4):
-            centred = fine_rows[:, :, g % 2, :, g // 2].reshape(CROWS, D1) - average
+            centred = fine_out[part, :, g % 2, :, g // 2].reshape(CROWS, D1) - average
             total = total + jnp.sum(centred * centred, axis=-1, keepdims=True)
         inverse = lax.rsqrt(total / (4 * D1) + EPS)
         for g in range(4):
             lanes = pl.ds(g * D1, D1)
-            centred = fine_rows[:, :, g % 2, :, g // 2].reshape(CROWS, D1) - average
+            centred = fine_out[part, :, g % 2, :, g // 2].reshape(CROWS, D1) - average
             merged[:, lanes] = (centred * inverse * gain_merge[:, lanes]).astype(jnp.bfloat16)
         coarse = dot(merged[...], w_merge[...]).astype(jnp.bfloat16)
         coarse_in[c] = coarse
@@ -344,7 +340,6 @@
         for k in (3, 2, 1):
             coarse_copy(c, k).start()
         coarse_recv[c, member] = coarse_send[c, member]
-        result_copy(1, c).start()
 
     def coarse_attention(c):
         @pl.when(c == 0)
@@ -381,9 +376,15 @@
         back_recv[c, member] = back_send[c, member]
 
     def finish(c):
+        @pl.when(c == 0)
+        def _():
+            loads[8].wait()
+
         for k in (1, 2, 3):
             back_copy(c, k).wait_recv()
-        result_copy(2, c).start()
+        rows = dot(cmaps[FROM_SEND], back_recv[c].reshape(CROWS, D2)).astype(jnp.bfloat16)
+        rows = dot(rows, w_out_coarse[...]) + coarse_in[c].astype(jnp.float32)
+        coarse_out[pl.ds(2 * c, 2)] = rows.reshape(2, HALF_R, HALF_C, LEVELS, D2)
 
     def step(s, _):
         for depth, stage in enumerate((fine_attention, merge, coarse_attention, finish)):
@@ -402,22 +403,9 @@
             heads_copy(c, k).wait_send()
             coarse_copy(c, k).wait_send()
             back_copy(c, k).wait_send()
-        for n in range(3):
-            result_copy(n, c).wait()
         return 0
 
     lax.fori_loop(0, n_chunks, drain, 0)
-
-
-def last_kernel(
-    tokens, heads, coarse_in, heads_coarse, w_out_fine, w_out_coarse, maps, fine_out, coarse_out
-):
-    fine = dot(heads[...].reshape(4 * CROWS, D1), w_out_fine[...])
-    fine = fine + tokens[...].reshape(4 * CROWS, D1).astype(jnp.float32)
-    fine_out[...] = fine.reshape(fine_out.shape)
-    rows = dot(maps[...], heads_coarse[...].reshape(CROWS, D2)).astype(jnp.bfloat16)
-    coarse = dot(rows, w_out_coarse[...]) + coarse_in[0].astype(jnp.float32)
-    coarse_out[...] = coarse.reshape(coarse_out.shape)
 
 
 def body(
@@ -439,20 +427,18 @@
     bf16, f32 = jnp.bfloat16, jnp.float32
     maps = jnp.asarray(pair_maps(), bf16)
     cmaps = jnp.asarray(coarse_maps(), bf16)
-    cmap_back = jnp.asarray(coarse_maps()[TO_SEND].T, bf16)
     hbm = pl.BlockSpec(memory_space=pl.ANY)
     vmem = pl.BlockSpec(memory_space=pltpu.VMEM)
     dma = pltpu.SemaphoreType.DMA
     slots = (chunks, NW, CROWS // NW // 4, 4, D2)
-    heads, coarse_in, heads_coarse = pl.pallas_call(
+    fine_out, coarse_out = pl.pallas_call(
         functools.partial(main_kernel, chunks, lax.axis_size("lat"), lax.axis_size("lon")),
         out_shape=(
-            jax.ShapeDtypeStruct(tokens.shape, bf16),
-            jax.ShapeDtypeStruct((chunks, CROWS, D2), bf16),
-            jax.ShapeDtypeStruct(slots, bf16),
+            pltpu.VMEM((batch, HALF_R, 2, HALF_C, 2, LEVELS, D1), f32),
+            pltpu.VMEM((batch, HALF_R, HALF_C, LEVELS, D2), f32),
         ),
-        in_specs=[hbm, vmem, hbm, hbm, hbm, vmem, hbm, vmem, hbm, hbm, hbm, hbm],
-        out_specs=(hbm, hbm, hbm),
+        in_specs=[hbm, vmem, hbm, hbm, hbm, vmem, hbm, vmem, hbm, hbm, hbm, hbm, hbm],
+        out_specs=(vmem, vmem),
         scratch_shapes=[
             pltpu.VMEM(tokens.shape, bf16),
             pltpu.VMEM(w_qkv_fine.shape, bf16),
@@ -461,6 +447,7 @@
             pltpu.VMEM(w_merge.shape, bf16),
             pltpu.VMEM(w_qkv_coarse.shape, bf16),
             pltpu.VMEM(bias_coarse.shape, f32),
+            pltpu.VMEM(w_out_coarse.shape, bf16),
             pltpu.VMEM(maps.shape, bf16),
             pltpu.VMEM(cmaps.shape, bf16),
             pltpu.VMEM((chunks, 4, 2, HALF_R, HALF_C, LEVELS, D1), bf16),
@@ -469,7 +456,6 @@
             pltpu.VMEM((NW * WIN, D1), bf16),
             pltpu.VMEM((chunks, 4, 2, HALF_R, HALF_C, LEVELS, D1), bf16),
             pltpu.VMEM(tokens.shape, bf16),
-            pltpu.VMEM((2, HALF_R, 2, HALF_C, 2, LEVELS, D1), f32),
             pltpu.VMEM((CROWS, 4 * D1), bf16),
             pltpu.VMEM((chunks, CROWS, D2), bf16),
             pltpu.VMEM(slots, bf16),
@@ -478,12 +464,11 @@
             pltpu.VMEM((WIN, 3 * D2), bf16),
             pltpu.VMEM(slots, bf16),
             pltpu.VMEM(slots, bf16),
-            dma((8,)),
+            dma((9,)),
             dma((chunks,)),
             dma((chunks,)),
         ]
-        + [dma((chunks, 4)) for _ in range(8)]
-        + [dma((3, chunks))],
+        + [dma((chunks, 4)) for _ in range(8)],
         compiler_params=pltpu.CompilerParams(
             collective_id=0, has_side_effects=True, vmem_limit_bytes=VMEM_LIMIT
         ),
@@ -501,33 +486,9 @@
         bias_coarse,
         maps,
         cmaps,
+        w_out_coarse,
     )
-    chunk3 = lambda c: (c, 0, 0)
-    chunk5 = lambda c: (c, 0, 0, 0, 0)
-    whole = lambda c: (0, 0)
-    fine_out, coarse_out = pl.pallas_call(
-        last_kernel,
-        grid=(chunks,),
-        out_shape=(
-            jax.ShapeDtypeStruct(tokens.shape, f32),
-            jax.ShapeDtypeStruct((batch, HALF_R, HALF_C, LEVELS, D2), f32),
-        ),
-        in_specs=[
-            pl.BlockSpec((2, ROWS, COLS, LEVELS, D1), chunk5),
-            pl.BlockSpec((2, ROWS, COLS, LEVELS, D1), chunk5),
-            pl.BlockSpec((1, CROWS, D2), chunk3),
-            pl.BlockSpec((1,) + slots[1:], chunk5),
-            pl.BlockSpec((D1, D1), whole),
-            pl.BlockSpec((D2, D2), whole),
-            pl.BlockSpec(cmap_back.shape, whole),
-        ],
-        out_specs=(
-            pl.BlockSpec((2, ROWS, COLS, LEVELS, D1), chunk5),
-            pl.BlockSpec((2, HALF_R, HALF_C, LEVELS, D2), chunk5),
-        ),
-        compiler_params=pltpu.CompilerParams(vmem_limit_bytes=VMEM_LIMIT),
-        name="last_projections",
-    )(tokens, heads, coarse_in, heads_coarse, w_out_fine, w_out_coarse, cmap_back)
+    fine_out = fine_out.reshape(tokens.shape)
     return fine_out.transpose(0, 3, 1, 2, 4), coarse_out.transpose(0, 3, 1, 2, 4)
 
 

time: 94 us -> 86.7 us (0.922)
  the two profiles are of different devices: /device:TPU:52 before, /device:TPU:42 now
where the time goes in v2:
time: 86.7 us; the launch traced here: 86.6 us
  Pallas kernels  82.3 us (95%)
  local copies, waits for them, and re-layouts  3.59 us (4%)
    pallas_call x1, Pallas kernels, body(): pl.pallas_call(functools.partial(main_kernel, chunks, lax.axis_size('lat'...  82.3 us
    unnamed x2, local copies, waits for them, and re-layouts  3.59 us

profile of v2, /device:TPU:42, one launch (start us, length us, event | category | flops | bytes accessed | tf_op | source)
XLA Modules:
  0.0 86.6 jit_solution(15541997304216158900)
XLA Ops:
  0.6 82.3 %window_levels.1 = (f32[8,3,2,6,2,4,512]{6,5,4,3,2,1,0:T(4,128)S(1)}, f32[8,3,6,4,1024]{4,3,2,1,0:T(4,128)S(1)}) custom-call(bf16[8,6,12,4,512]{4,3,2,1,0:T(4,128)(2,1)} %bitcast.10, f32[1,512]{1,0:T(1,128)} %bitcast.13, bf16[512,1536]{1,0:T(8,128)(2,1)} %w_qkv_fine_hbm.1, f32[8,144,144]{2,1,0:T(8,128)} %bias_fine_hbm.1, bf16[512,512]{1,0:T(8,128)(2,1)} %w_out_fine_hbm.1, ...), custom_call_target="tpu_custom_call" | custom-call | tf_op jit(solution)/shard_map/window_levels/pallas_call | solution.py:434
  83.0 2.2 %copy.17 = f32[8,4,6,12,512]{4,1,3,2,0:T(4,128)} copy(f32[8,4,6,12,512]{4,1,3,2,0:T(4,128)S(1)} %bitcast.8) | data formatting | bytes 9437184
  85.2 1.4 %copy.18 = f32[8,4,3,6,1024]{4,1,3,2,0:T(4,128)} copy(f32[8,4,3,6,1024]{4,1,3,2,0:T(4,128)S(1)} %bitcast.9) | data formatting | bytes 4718592

commit v3 on v2

--- a/solution.py
+++ b/solution.py
@@ -15,6 +15,7 @@
 WIN = WLEV * ROWS * COLS
 PAIR = 2 * WIN
 NW = 4
+BEHIND = (0, 2, 4, 5)
 AHEAD = 2
 CROWS = 2 * HALF_R * HALF_C * LEVELS
 D1, D2 = 512, 1024
@@ -387,7 +388,7 @@
         coarse_out[pl.ds(2 * c, 2)] = rows.reshape(2, HALF_R, HALF_C, LEVELS, D2)
 
     def step(s, _):
-        for depth, stage in enumerate((fine_attention, merge, coarse_attention, finish)):
+        for depth, stage in zip(BEHIND, (fine_attention, merge, coarse_attention, finish)):
 
             @pl.when((s >= depth) & (s < n_chunks + depth))
             def _():
@@ -395,7 +396,7 @@
 
         return 0
 
-    lax.fori_loop(0, n_chunks + 3, step, 0)
+    lax.fori_loop(0, n_chunks + BEHIND[-1], step, 0)
 
     def drain(c, _):
         for k in (1, 2, 3):

time: 86.7 us -> 83.6 us (0.964)
  the two profiles are of different devices: /device:TPU:42 before, /device:TPU:1 now
where the time goes in v3:
time: 83.6 us; the launch traced here: 83.4 us
  Pallas kernels  79.2 us (95%)
  local copies, waits for them, and re-layouts  3.59 us (4%)
    pallas_call x1, Pallas kernels, body(): pl.pallas_call(functools.partial(main_kernel, chunks, lax.axis_size('lat'...  79.2 us
    unnamed x2, local copies, waits for them, and re-layouts  3.59 us

profile of v3, /device:TPU:1, one launch (start us, length us, event | category | flops | bytes accessed | tf_op | source)
XLA Modules:
  0.0 83.4 jit_solution(5650932490492871929)
XLA Ops:
  0.6 79.2 %window_levels.1 = (f32[8,3,2,6,2,4,512]{6,5,4,3,2,1,0:T(4,128)S(1)}, f32[8,3,6,4,1024]{4,3,2,1,0:T(4,128)S(1)}) custom-call(bf16[8,6,12,4,512]{4,3,2,1,0:T(4,128)(2,1)} %bitcast.10, f32[1,512]{1,0:T(1,128)} %bitcast.13, bf16[512,1536]{1,0:T(8,128)(2,1)} %w_qkv_fine_hbm.1, f32[8,144,144]{2,1,0:T(8,128)} %bias_fine_hbm.1, bf16[512,512]{1,0:T(8,128)(2,1)} %w_out_fine_hbm.1, ...), custom_call_target="tpu_custom_call" | custom-call | tf_op jit(solution)/shard_map/window_levels/pallas_call | solution.py:435
  79.9 2.2 %copy.17 = f32[8,4,6,12,512]{4,1,3,2,0:T(4,128)} copy(f32[8,4,6,12,512]{4,1,3,2,0:T(4,128)S(1)} %bitcast.8) | data formatting | bytes 9437184
  82.0 1.4 %copy.18 = f32[8,4,3,6,1024]{4,1,3,2,0:T(4,128)} copy(f32[8,4,3,6,1024]{4,1,3,2,0:T(4,128)S(1)} %bitcast.9) | data formatting | bytes 4718592

commit v4 on v3

--- a/solution.py
+++ b/solution.py
@@ -71,19 +71,20 @@
     return (centred * lax.rsqrt(variance + EPS) * gain).astype(jnp.bfloat16)
 
 
-def attend_pair(query, key, value, bias0, bias1):
+def attend_all(queries, keys, values, biases):
     low = lax.broadcasted_iota(jnp.int32, (WIN, 128), 1) < HS
-    one = jnp.ones((), jnp.bfloat16)
     zero = jnp.zeros((), jnp.bfloat16)
-    results = []
-    for side, bias in ((low, bias0), (jnp.logical_not(low), bias1)):
-        scores = dot_t(jnp.where(side, query, zero), key) + bias
-        top = jnp.max(scores, axis=-1, keepdims=True)
-        probs = jnp.exp(scores - top).astype(jnp.bfloat16)
-        results.append(dot(probs, jnp.where(side, value, one)))
-    total = jnp.where(low, results[0], results[1])
-    weight = pltpu.roll(jnp.where(low, results[1], results[0]), HS, 1)
-    return (total / weight).astype(jnp.bfloat16)
+    ones = jnp.ones((WIN, 128), jnp.bfloat16)
+    scores = [
+        dot_t(jnp.concatenate([jnp.where(low, q, zero), jnp.where(low, zero, q)], axis=0), k)
+        for q, k in zip(queries, keys)
+    ]
+    scores = [s + b for s, b in zip(scores, biases)]
+    probs = [jnp.exp(s - jnp.max(s, axis=-1, keepdims=True)).astype(jnp.bfloat16) for s in scores]
+    sums = [dot(p, jnp.concatenate([v, ones], axis=1)) for p, v in zip(probs, values)]
+    both = jnp.concatenate([low, low], axis=1)
+    picked = [jnp.where(both, s[:WIN], s[WIN:]) for s in sums]
+    return [(p[:, :128] / p[:, 128:]).astype(jnp.bfloat16) for p in picked]
 
 
 def main_kernel(
@@ -286,18 +287,16 @@
 
         def window(w, _):
             rows = pl.ds(pl.multiple_of(w * WIN, 16), WIN)
-            for pair in range(D1 // 128):
-                lanes = [pl.ds(n * D1 + pair * 128, 128) for n in range(3)]
-                win_heads[rows, lanes[0]] = attend_pair(
-                    qkv[rows, lanes[0]],
-                    qkv[rows, lanes[1]],
-                    qkv[rows, lanes[2]],
-                    bias_fine[which, 2 * pair],
-                    bias_fine[which, 2 * pair + 1],
-                )
+            lanes = [[pl.ds(n * D1 + p * 128, 128) for p in range(D1 // 128)] for n in range(3)]
+            results = attend_all(
+                *([qkv[rows, lane] for lane in group] for group in lanes),
+                [bias_fine[which, pl.ds(2 * p, 2)].reshape(2 * WIN, WIN) for p in range(D1 // 128)],
+            )
+            for lane, result in zip(lanes[0], results):
+                win_heads[rows, lane] = result
             return 0
 
-        lax.fori_loop(0, NW, window, 0)
+        lax.fori_loop(0, NW, window, 0, unroll=2)
         for b in range(2):
             rows = dot(maps[1], win_heads[pl.ds(b * PAIR, PAIR)]).astype(jnp.bfloat16)
             heads_send[c, :, b] = rows.reshape(4, HALF_R, HALF_C, LEVELS, D1)
@@ -359,16 +358,12 @@
                 part = part * jnp.bfloat16(HS**-0.5)
             qkv_coarse[:, lanes] = part
         results = []
-        for pair in range(D2 // 128):
-            lanes = [pl.ds(n * D2 + pair * 128, 128) for n in range(3)]
-            results.append(
-                attend_pair(
-                    qkv_coarse[:, lanes[0]],
-                    qkv_coarse[:, lanes[1]],
-                    qkv_coarse[:, lanes[2]],
-                    bias_coarse[2 * pair],
-                    bias_coarse[2 * pair + 1],
-                )
+        for first in range(0, D2 // 128, 4):
+            pairs = range(first, first + 4)
+            lanes = [[pl.ds(n * D2 + p * 128, 128) for p in pairs] for n in range(3)]
+            results += attend_all(
+                *([qkv_coarse[:, lane] for lane in group] for group in lanes),
+                [bias_coarse[pl.ds(2 * p, 2)].reshape(2 * WIN, WIN) for p in pairs],
             )
         rows = dot(cmaps[FROM_WIN], jnp.concatenate(results, axis=1)).astype(jnp.bfloat16)
         back_send[c] = rows.reshape(back_send.shape[1:])

time: 83.6 us -> 82.2 us (0.983)
  Pallas kernels: 79.2 us -> 77.8 us
    pallas_call x1, Pallas kernels: 79.2 us -> 77.8 us  [body(): pl.pallas_call(functools.partial(main_kernel, chunks, lax.axis_size('lat'...]
where the time goes in v4:
time: 82.2 us; the launch traced here: 82 us
  Pallas kernels  77.8 us (95%)
  local copies, waits for them, and re-layouts  3.59 us (4%)
    pallas_call x1, Pallas kernels, body(): pl.pallas_call(functools.partial(main_kernel, chunks, lax.axis_size('lat'...  77.8 us
    unnamed x2, local copies, waits for them, and re-layouts  3.59 us

profile of v4, /device:TPU:1, one launch (start us, length us, event | category | flops | bytes accessed | tf_op | source)
XLA Modules:
  0.0 82.0 jit_solution(8996634830239940226)
XLA Ops:
  0.6 77.8 %window_levels.1 = (f32[8,3,2,6,2,4,512]{6,5,4,3,2,1,0:T(4,128)S(1)}, f32[8,3,6,4,1024]{4,3,2,1,0:T(4,128)S(1)}) custom-call(bf16[8,6,12,4,512]{4,3,2,1,0:T(4,128)(2,1)} %bitcast.10, f32[1,512]{1,0:T(1,128)} %bitcast.13, bf16[512,1536]{1,0:T(8,128)(2,1)} %w_qkv_fine_hbm.1, f32[8,144,144]{2,1,0:T(8,128)} %bias_fine_hbm.1, bf16[512,512]{1,0:T(8,128)(2,1)} %w_out_fine_hbm.1, ...), custom_call_target="tpu_custom_call" | custom-call | tf_op jit(solution)/shard_map/window_levels/pallas_call | solution.py:430
  78.4 2.2 %copy.17 = f32[8,4,6,12,512]{4,1,3,2,0:T(4,128)} copy(f32[8,4,6,12,512]{4,1,3,2,0:T(4,128)S(1)} %bitcast.8) | data formatting | bytes 9437184
  80.6 1.4 %copy.18 = f32[8,4,3,6,1024]{4,1,3,2,0:T(4,128)} copy(f32[8,4,3,6,1024]{4,1,3,2,0:T(4,128)S(1)} %bitcast.9) | data formatting | bytes 4718592

commit v5 on v4

--- a/solution.py
+++ b/solution.py
@@ -15,7 +15,7 @@
 WIN = WLEV * ROWS * COLS
 PAIR = 2 * WIN
 NW = 4
-BEHIND = (0, 2, 4, 5)
+BEHIND = (0, 1, 3, 5)
 AHEAD = 2
 CROWS = 2 * HALF_R * HALF_C * LEVELS
 D1, D2 = 512, 1024

time: 82.2 us -> 78.3 us (0.953)
  the two profiles are of different devices: /device:TPU:1 before, /device:TPU:42 now
where the time goes in v5:
time: 78.3 us; the launch traced here: 77.8 us
  Pallas kernels  73.6 us (94%)
  local copies, waits for them, and re-layouts  3.59 us (5%)
    pallas_call x1, Pallas kernels, body(): pl.pallas_call(functools.partial(main_kernel, chunks, lax.axis_size('lat'...  73.6 us
    unnamed x2, local copies, waits for them, and re-layouts  3.59 us

profile of v5, /device:TPU:42, one launch (start us, length us, event | category | flops | bytes accessed | tf_op | source)
XLA Modules:
  0.0 77.8 jit_solution(16072209208241275777)
XLA Ops:
  0.6 73.6 %window_levels.1 = (f32[8,3,2,6,2,4,512]{6,5,4,3,2,1,0:T(4,128)S(1)}, f32[8,3,6,4,1024]{4,3,2,1,0:T(4,128)S(1)}) custom-call(bf16[8,6,12,4,512]{4,3,2,1,0:T(4,128)(2,1)} %bitcast.10, f32[1,512]{1,0:T(1,128)} %bitcast.13, bf16[512,1536]{1,0:T(8,128)(2,1)} %w_qkv_fine_hbm.1, f32[8,144,144]{2,1,0:T(8,128)} %bias_fine_hbm.1, bf16[512,512]{1,0:T(8,128)(2,1)} %w_out_fine_hbm.1, ...), custom_call_target="tpu_custom_call" | custom-call | tf_op jit(solution)/shard_map/window_levels/pallas_call | solution.py:430
  74.2 2.2 %copy.17 = f32[8,4,6,12,512]{4,1,3,2,0:T(4,128)} copy(f32[8,4,6,12,512]{4,1,3,2,0:T(4,128)S(1)} %bitcast.8) | data formatting | bytes 9437184
  76.4 1.4 %copy.18 = f32[8,4,3,6,1024]{4,1,3,2,0:T(4,128)} copy(f32[8,4,3,6,1024]{4,1,3,2,0:T(4,128)S(1)} %bitcast.9) | data formatting | bytes 4718592

commit v6 on v5

--- a/solution.py
+++ b/solution.py
@@ -296,7 +296,7 @@
                 win_heads[rows, lane] = result
             return 0
 
-        lax.fori_loop(0, NW, window, 0, unroll=2)
+        lax.fori_loop(0, NW, window, 0, unroll=4)
         for b in range(2):
             rows = dot(maps[1], win_heads[pl.ds(b * PAIR, PAIR)]).astype(jnp.bfloat16)
             heads_send[c, :, b] = rows.reshape(4, HALF_R, HALF_C, LEVELS, D1)

time: 78.3 us -> 77.5 us (0.990)
  Pallas kernels: 73.6 us -> 72.8 us
where the time goes in v6:
time: 77.5 us; the launch traced here: 77.1 us
  Pallas kernels  72.8 us (94%)
  local copies, waits for them, and re-layouts  3.59 us (5%)
    pallas_call x1, Pallas kernels, body(): pl.pallas_call(functools.partial(main_kernel, chunks, lax.axis_size('lat'...  72.8 us
    unnamed x2, local copies, waits for them, and re-layouts  3.59 us

profile of v6, /device:TPU:42, one launch (start us, length us, event | category | flops | bytes accessed | tf_op | source)
XLA Modules:
  0.0 77.1 jit_solution(721882906484418781)
XLA Ops:
  0.6 72.8 %window_levels.1 = (f32[8,3,2,6,2,4,512]{6,5,4,3,2,1,0:T(4,128)S(1)}, f32[8,3,6,4,1024]{4,3,2,1,0:T(4,128)S(1)}) custom-call(bf16[8,6,12,4,512]{4,3,2,1,0:T(4,128)(2,1)} %bitcast.10, f32[1,512]{1,0:T(1,128)} %bitcast.13, bf16[512,1536]{1,0:T(8,128)(2,1)} %w_qkv_fine_hbm.1, f32[8,144,144]{2,1,0:T(8,128)} %bias_fine_hbm.1, bf16[512,512]{1,0:T(8,128)(2,1)} %w_out_fine_hbm.1, ...), custom_call_target="tpu_custom_call" | custom-call | tf_op jit(solution)/shard_map/window_levels/pallas_call | solution.py:430
  73.5 2.2 %copy.17 = f32[8,4,6,12,512]{4,1,3,2,0:T(4,128)} copy(f32[8,4,6,12,512]{4,1,3,2,0:T(4,128)S(1)} %bitcast.8) | data formatting | bytes 9437184
  75.7 1.4 %copy.18 = f32[8,4,3,6,1024]{4,1,3,2,0:T(4,128)} copy(f32[8,4,3,6,1024]{4,1,3,2,0:T(4,128)S(1)} %bitcast.9) | data formatting | bytes 4718592
